TPU v7x, 256 devices: a whole 4x4x8 slice. The times are simulated.
256 devices in a mesh: pair: 8 (over x, core), section: 32 (over z, y).
Axes of the slice: x: 4, y: 4, z: 8, core: 2. Of those that a mesh axis runs over, the one named last changes fastest.
Arguments:
- queries: bfloat16 [8, 4096, 4096], P('pair', 'section'), may hold values from -160 to 160
- keys: bfloat16 [8, 4096, 512], P('pair', 'section'), may hold values from -6 to 6
- values: bfloat16 [8, 4096, 512], P('pair', 'section'), may hold values from -6 to 6
- prefix_keys: bfloat16 [256, 512], P('section'), may hold values from -6 to 6
- prefix_values: bfloat16 [256, 512], P('section'), may hold values from -6 to 6
- lengths: int32 [8], replicated, may hold values from 512 to 4096, as said below
- partner: int32 [8], replicated, may hold values from 0 to 7, as said below
Outputs:
- first_order: bfloat16 [8, 4096, 4096], P('pair', 'section')
- second_order: bfloat16 [8, 4096, 4096], P('pair', 'section')
Inputs may be any that keep to these rules, and one draw needn't show every extreme that they name: `lengths`: one response has exactly 4096 tokens. partner[r] = r xor m for one m from 1 to 7 common to the whole list, so partner[partner[r]] = r.
All inputs are finite; a program needn't handle non-finite values.
Results may differ from a plain program's by a relative error of at most 0.018.
Values may be sent and summed in bfloat16 or wider, within the bound.
A program may use at most 128 MiB of HBM per device.

v0:
```python
import functools
import math

import jax
import jax.numpy as jnp
from jax import lax
from jax.sharding import PartitionSpec as P

QH = 32
KVH = 4
DH = 128


NEGATIVE = -1e30
block_keys = 512


def as_sent(value):

    def short(part):
        return part.astype(jnp.bfloat16) if part.dtype == jnp.float32 else part

    return jax.tree.map(short, value)


def partner_2(block, axis, bit):
    count = lax.axis_size(axis)
    route = []
    for low in range(count):
        high = low | 1 << bit
        if high != low and high < count:
            route += [(low, high), (high, low)]
    return lax.ppermute(block, axis, route)


def empty_state(rows_here):
    return (
        jnp.full((KVH, QH // KVH, rows_here), NEGATIVE, jnp.float32),
        jnp.zeros((KVH, QH // KVH, rows_here), jnp.float32),
        jnp.zeros((KVH, QH // KVH, rows_here, DH), jnp.float32),
    )


def absorb(carry_state, query_heads, key_block, value_block, allowed):
    running_max, weight_total, weighted = carry_state
    key_count = key_block.shape[0]
    key_heads = key_block.reshape(key_count, KVH, DH)
    value_heads = value_block.reshape(key_count, KVH, DH)
    scores = jnp.einsum(
        "qkgd,skd->kgqs", query_heads, key_heads, preferred_element_type=jnp.float32
    ) * DH ** (-0.5)
    scores = jnp.where(allowed, scores, NEGATIVE)
    new_max = jnp.maximum(running_max, jnp.max(scores, axis=-1))
    fading = jnp.exp(running_max - new_max)
    weights = jnp.where(allowed, jnp.exp(scores - new_max[..., None]), 0.0)
    weight_total = weight_total * fading + jnp.sum(weights, axis=-1)
    weighted = weighted * fading[..., None] + jnp.einsum(
        "kgqs,skd->kgqd",
        weights.astype(jnp.bfloat16),
        value_heads,
        preferred_element_type=jnp.float32,
    )
    return (new_max, weight_total, weighted)


def absorb_range(carry_state, query_heads, key_block, value_block, first_index, limit, allowed_of):
    key_count = key_block.shape[0]
    span_rows = key_count if key_count <= block_keys else math.gcd(key_count, block_keys)

    def one_span(span_index, carried):
        offset = span_index * span_rows
        key_part = lax.dynamic_slice_in_dim(key_block, offset, span_rows, 0)
        value_part = lax.dynamic_slice_in_dim(value_block, offset, span_rows, 0)
        first_key = first_index + offset
        positions = first_key + jnp.arange(span_rows, dtype=jnp.int32)
        return lax.cond(
            first_key < limit,
            lambda current: absorb(
                current, query_heads, key_part, value_part, allowed_of(positions)
            ),
            lambda current: current,
            carried,
        )

    return lax.fori_loop(0, key_count // span_rows, one_span, carry_state)


def finish(carry_state, valid_rows):
    mixture = carry_state[2] / carry_state[1][..., None]
    flattened = mixture.transpose(2, 0, 1, 3).reshape(mixture.shape[2], QH * DH)
    return jnp.where(valid_rows[:, None], flattened, 0.0).astype(jnp.bfloat16)[None]


def xor_route(payload, distance, slot_count, swap_once):
    bit_count = slot_count.bit_length() - 1

    def along_bits(pattern, carried):
        for bit_index in range(bit_count):
            if pattern >> bit_index & 1:
                carried = swap_once(carried, bit_index)
        return carried

    branches = [functools.partial(along_bits, pattern) for pattern in range(1, slot_count)]
    return lax.switch(distance - 1, branches, payload)


def local(queries, keys, values, prefix_keys, prefix_values, lengths, partner):
    own_slot = lax.axis_index("pair")
    section_index = lax.axis_index("section")
    slot_count = lax.axis_size("pair")
    rows_here = queries.shape[1]
    query_heads = queries[0].reshape(rows_here, KVH, QH // KVH, DH)
    query_rows = section_index * rows_here + jnp.arange(rows_here, dtype=jnp.int32)
    own_length = lengths[own_slot]
    partner_slot = partner[own_slot]
    partner_length = lengths[partner_slot]
    distance = jnp.bitwise_xor(partner_slot, own_slot)
    row_limit = section_index * rows_here + rows_here

    def allow_every(positions):
        return jnp.ones((rows_here, positions.shape[0]), jnp.bool_)

    def causal(positions):
        return positions[None, :] <= query_rows[:, None]

    def within_partner(positions):
        return jnp.broadcast_to(
            positions[None, :] < partner_length, (rows_here, positions.shape[0])
        )

    pieces = (
        lax.all_gather(prefix_keys, "section", axis=0, tiled=True),
        lax.all_gather(prefix_values, "section", axis=0, tiled=True),
    )
    first_index = jnp.int32(0)
    prompt_state = absorb_range(
        empty_state(rows_here),
        query_heads,
        pieces[0],
        pieces[1],
        first_index,
        first_index + pieces[0].shape[0],
        allow_every,
    )
    own_keys = keys[0]
    own_values = values[0]
    pieces = (
        lax.all_gather(own_keys, "section", axis=0, tiled=True),
        lax.all_gather(own_values, "section", axis=0, tiled=True),
    )
    own_state = absorb_range(
        prompt_state, query_heads, pieces[0], pieces[1], jnp.int32(0), row_limit, causal
    )
    stacked = xor_route(
        jnp.stack([own_keys, own_values]),
        distance,
        slot_count,
        lambda carried, bit_index: jax.tree.map(
            lambda part, own: part.astype(own.dtype),
            partner_2(as_sent(carried), "pair", bit_index),
            carried,
        ),
    )
    partner_keys = stacked[0]
    partner_values = stacked[1]
    pieces = (
        lax.all_gather(as_sent(partner_keys), "section", axis=0, tiled=True),
        lax.all_gather(as_sent(partner_values), "section", axis=0, tiled=True),
    )
    both_state = absorb_range(
        own_state, query_heads, pieces[0], pieces[1], jnp.int32(0), partner_length, within_partner
    )
    valid_rows = query_rows < own_length
    return (finish(own_state, valid_rows), finish(both_state, valid_rows))


def solution(mesh):
    in_specs = (
        P("pair", "section", None),
        P("pair", "section", None),
        P("pair", "section", None),
        P("section", None),
        P("section", None),
        P(),
        P(),
    )
    out_specs = (P("pair", "section", None), P("pair", "section", None))
    return jax.shard_map(local, mesh=mesh, in_specs=in_specs, out_specs=out_specs, check_vma=False)
```

profile of v0, /device:TPU:18, one launch (start us, length us, event | category | flops | bytes accessed | tf_op | source)
XLA Modules:
  0.0 456.4 jit_solution(17328873172117474313)
XLA Ops:
  7.2 1.7 copy.48
  9.0 1.7 copy.49
  10.7 1.2 dynamic_slice.66
  12.5 1.0 pad_maximum_fusion
  13.5 1.8 conditional.3
  13.6 1.7 collective-permute-done
  15.3 1.0 fusion.38
  19.0 1.6 copy.42
  20.6 51.7 %all_gather.18 = bf16[256,512]{1,0:T(8,128)(2,1)S(1)} all-gather(bf16[8,512]{1,0:T(8,128)(2,1)S(1)} %copy-done.1), channel_id=1, replica_groups=mesh['pair'=8,'section'=32] {'section'}, dimensions={0}, use_global_device_ids=true | all-gather | bytes 270336 | tf_op jit(solution)/shard_map/all_gather | solution.py:132
  72.5 47.3 %all_gather.19 = bf16[256,512]{1,0:T(8,128)(2,1)S(1)} all-gather(bf16[8,512]{1,0:T(8,128)(2,1)S(1)} %copy-done.2), channel_id=1, replica_groups=mesh['pair'=8,'section'=32] {'section'}, dimensions={0}, use_global_device_ids=true | all-gather | bytes 270336 | tf_op jit(solution)/shard_map/all_gather | solution.py:133
  124.0 1.8 fusion.33
  125.9 58.9 %all-gather.11.cloned.1.call-done = bf16[1,4096,512]{1,2,0:T(8,128)(2,1)} async-done(((bf16[1,128,512]{1,2,0:T(8,128)(2,1)}), bf16[1,4096,512]{1,2,0:T(8,128)(2,1)}) %all-gather.11.cloned.1.call-update) | async-done | bytes 4194320 | tf_op jit(solution)/shard_map/all_gather | solution.py:149
  184.8 9.0 %while.43 = (s32[]{:T(128)}, f32[4,8,128]{2,1,0:T(8,128)S(1)}, f32[4,8,128]{2,1,0:T(8,128)S(1)}, f32[4,8,128,128]{3,2,1,0:T(8,128)S(1)}, s32[]{:T(128)}, /*index...) while((s32[]{:T(128)}, f32[4,8,128]{2,1,0:T(8,128)S(1)}, ...), condition=%wide.region_7.0_spmd.clone, body=%wide.region_2.7_spmd.clone.sunk | while | flops 1102127744 | bytes 34089280 | solution.py:85
  184.8 8.5 %conditional.8 = ((f32[4,8,128]{2,1,0:T(8,128)S(1)}, f32[4,8,128]{2,1,0:T(8,128)S(1)}, f32[4,8,128,128]{3,2,1,0:T(8,128)S(1)})) conditional(s32[]{:T(128)} %convert_element_type.73, (f32[4,8,128]{2,1,0:T(8,128)S(1)}, f32[4,8,128]{2,1,0:T(8,128)S(1)}, f32[4,8,128,128]{3,2,1,0:T(8,128)S(1)}) %tuple.139, (s32[]{:T(128)}, s32[512]{0:T(512)S(1)}, ...), branch_computations={%region_3.0_spmd, %region_4.6_spmd} | conditional | flops 1102127744 | bytes 34086480 | solution.py:76
  184.8 1.3 constant_dynamic-slice_fusion
  186.2 1.5 fusion.2
  187.7 2.1 fusion.4
  189.8 3.4 multiply_add_fusion
  194.5 1.6 copy.51
  196.1 2.3 reshape.125
  198.4 72.2 %all-gather.13.cloned.1.call-done = bf16[1,4096,512]{1,2,0:T(8,128)(2,1)} async-done(((bf16[1,128,512]{1,2,0:T(8,128)(2,1)}), bf16[1,4096,512]{1,2,0:T(8,128)(2,1)}) %all-gather.13.cloned.1.call-update) | async-done | bytes 4194320 | tf_op jit(solution)/shard_map/all_gather | solution.py:167
  270.6 85.7 %all-gather.15.cloned.1.call-done = bf16[1,4096,512]{1,2,0:T(8,128)(2,1)} async-done(((bf16[1,128,512]{1,2,0:T(8,128)(2,1)}), bf16[1,4096,512]{1,2,0:T(8,128)(2,1)}) %all-gather.15.cloned.1.call-update) | async-done | bytes 4194320 | tf_op jit(solution)/shard_map/all_gather | solution.py:168
  356.3 89.8 %while.42 = (s32[]{:T(128)}, f32[4,8,128]{2,1,0:T(8,128)S(1)}, f32[4,8,128]{2,1,0:T(8,128)S(1)}, f32[4,8,128,128]{3,2,1,0:T(8,128)S(1)}, s32[]{:T(128)}, /*index...) while((s32[]{:T(128)}, f32[4,8,128]{2,1,0:T(8,128)S(1)}, ...), condition=%wide.region_20.21_spmd, body=%wide.region_15.20_spmd.sunk | while | flops 1102062592 | bytes 33823024 | solution.py:85
  356.9 10.6 %conditional.7 = ((f32[4,8,128]{2,1,0:T(8,128)S(1)}, f32[4,8,128]{2,1,0:T(8,128)S(1)}, f32[4,8,128,128]{3,2,1,0:T(8,128)S(1)})) conditional(s32[]{:T(128)} %convert_element_type.72, (f32[4,8,128]{2,1,0:T(8,128)S(1)}, f32[4,8,128]{2,1,0:T(8,128)S(1)}, f32[4,8,128,128]{3,2,1,0:T(8,128)S(1)}) %tuple.136, (s32[]{:T(128)}, s32[512]{0:T(512)S(1)}, ...), branch_computations={%region_16.16_spmd, %region_17.19_spmd} | conditional | flops 1102062592 | bytes 33820752 | solution.py:76
  356.9 1.3 constant_dynamic-slice_fusion.2
  358.7 2.1 bitcast_reduce_fusion
  360.9 2.4 fusion.16
  363.3 4.2 multiply_add_fusion.2
  368.1 10.6 %conditional.7 = ((f32[4,8,128]{2,1,0:T(8,128)S(1)}, f32[4,8,128]{2,1,0:T(8,128)S(1)}, f32[4,8,128,128]{3,2,1,0:T(8,128)S(1)})) conditional(s32[]{:T(128)} %convert_element_type.72, (f32[4,8,128]{2,1,0:T(8,128)S(1)}, f32[4,8,128]{2,1,0:T(8,128)S(1)}, f32[4,8,128,128]{3,2,1,0:T(8,128)S(1)}) %tuple.136, (s32[]{:T(128)}, s32[512]{0:T(512)S(1)}, ...), branch_computations={%region_16.16_spmd, %region_17.19_spmd} | conditional | flops 1102062592 | bytes 33820752 | solution.py:76
  368.1 1.3 constant_dynamic-slice_fusion.2
  369.9 2.1 bitcast_reduce_fusion
  372.1 2.4 fusion.16
  374.5 4.2 multiply_add_fusion.2
  379.3 10.6 %conditional.7 = ((f32[4,8,128]{2,1,0:T(8,128)S(1)}, f32[4,8,128]{2,1,0:T(8,128)S(1)}, f32[4,8,128,128]{3,2,1,0:T(8,128)S(1)})) conditional(s32[]{:T(128)} %convert_element_type.72, (f32[4,8,128]{2,1,0:T(8,128)S(1)}, f32[4,8,128]{2,1,0:T(8,128)S(1)}, f32[4,8,128,128]{3,2,1,0:T(8,128)S(1)}) %tuple.136, (s32[]{:T(128)}, s32[512]{0:T(512)S(1)}, ...), branch_computations={%region_16.16_spmd, %region_17.19_spmd} | conditional | flops 1102062592 | bytes 33820752 | solution.py:76
  379.3 1.3 constant_dynamic-slice_fusion.2
  381.2 2.1 bitcast_reduce_fusion
  383.3 2.4 fusion.16
  385.8 4.2 multiply_add_fusion.2
  390.5 10.6 %conditional.7 = ((f32[4,8,128]{2,1,0:T(8,128)S(1)}, f32[4,8,128]{2,1,0:T(8,128)S(1)}, f32[4,8,128,128]{3,2,1,0:T(8,128)S(1)})) conditional(s32[]{:T(128)} %convert_element_type.72, (f32[4,8,128]{2,1,0:T(8,128)S(1)}, f32[4,8,128]{2,1,0:T(8,128)S(1)}, f32[4,8,128,128]{3,2,1,0:T(8,128)S(1)}) %tuple.136, (s32[]{:T(128)}, s32[512]{0:T(512)S(1)}, ...), branch_computations={%region_16.16_spmd, %region_17.19_spmd} | conditional | flops 1102062592 | bytes 33820752 | solution.py:76
  390.6 1.3 constant_dynamic-slice_fusion.2
  392.4 2.1 bitcast_reduce_fusion
  394.5 2.4 fusion.16
  397.0 4.2 multiply_add_fusion.2
  401.8 10.6 %conditional.7 = ((f32[4,8,128]{2,1,0:T(8,128)S(1)}, f32[4,8,128]{2,1,0:T(8,128)S(1)}, f32[4,8,128,128]{3,2,1,0:T(8,128)S(1)})) conditional(s32[]{:T(128)} %convert_element_type.72, (f32[4,8,128]{2,1,0:T(8,128)S(1)}, f32[4,8,128]{2,1,0:T(8,128)S(1)}, f32[4,8,128,128]{3,2,1,0:T(8,128)S(1)}) %tuple.136, (s32[]{:T(128)}, s32[512]{0:T(512)S(1)}, ...), branch_computations={%region_16.16_spmd, %region_17.19_spmd} | conditional | flops 1102062592 | bytes 33820752 | solution.py:76
  401.8 1.3 constant_dynamic-slice_fusion.2
  403.6 2.1 bitcast_reduce_fusion
  405.8 2.4 fusion.16
  408.2 4.2 multiply_add_fusion.2
  413.0 10.6 %conditional.7 = ((f32[4,8,128]{2,1,0:T(8,128)S(1)}, f32[4,8,128]{2,1,0:T(8,128)S(1)}, f32[4,8,128,128]{3,2,1,0:T(8,128)S(1)})) conditional(s32[]{:T(128)} %convert_element_type.72, (f32[4,8,128]{2,1,0:T(8,128)S(1)}, f32[4,8,128]{2,1,0:T(8,128)S(1)}, f32[4,8,128,128]{3,2,1,0:T(8,128)S(1)}) %tuple.136, (s32[]{:T(128)}, s32[512]{0:T(512)S(1)}, ...), branch_computations={%region_16.16_spmd, %region_17.19_spmd} | conditional | flops 1102062592 | bytes 33820752 | solution.py:76
  413.0 1.3 constant_dynamic-slice_fusion.2
  414.8 2.1 bitcast_reduce_fusion
  417.0 2.4 fusion.16
  419.4 4.2 multiply_add_fusion.2
  424.2 10.6 %conditional.7 = ((f32[4,8,128]{2,1,0:T(8,128)S(1)}, f32[4,8,128]{2,1,0:T(8,128)S(1)}, f32[4,8,128,128]{3,2,1,0:T(8,128)S(1)})) conditional(s32[]{:T(128)} %convert_element_type.72, (f32[4,8,128]{2,1,0:T(8,128)S(1)}, f32[4,8,128]{2,1,0:T(8,128)S(1)}, f32[4,8,128,128]{3,2,1,0:T(8,128)S(1)}) %tuple.136, (s32[]{:T(128)}, s32[512]{0:T(512)S(1)}, ...), branch_computations={%region_16.16_spmd, %region_17.19_spmd} | conditional | flops 1102062592 | bytes 33820752 | solution.py:76
  424.2 1.3 constant_dynamic-slice_fusion.2
  426.1 2.1 bitcast_reduce_fusion
  428.2 2.4 fusion.16
  430.7 4.2 multiply_add_fusion.2
  435.4 10.6 %conditional.7 = ((f32[4,8,128]{2,1,0:T(8,128)S(1)}, f32[4,8,128]{2,1,0:T(8,128)S(1)}, f32[4,8,128,128]{3,2,1,0:T(8,128)S(1)})) conditional(s32[]{:T(128)} %convert_element_type.72, (f32[4,8,128]{2,1,0:T(8,128)S(1)}, f32[4,8,128]{2,1,0:T(8,128)S(1)}, f32[4,8,128,128]{3,2,1,0:T(8,128)S(1)}) %tuple.136, (s32[]{:T(128)}, s32[512]{0:T(512)S(1)}, ...), branch_computations={%region_16.16_spmd, %region_17.19_spmd} | conditional | flops 1102062592 | bytes 33820752 | solution.py:76
  435.5 1.3 constant_dynamic-slice_fusion.2
  437.3 2.1 bitcast_reduce_fusion
  439.4 2.4 fusion.16
  441.9 4.2 multiply_add_fusion.2
  448.0 1.8 select_convert_fusion
  (102 shorter events, 13.2 us)
Async XLA Ops:
  7.2 13.4 %copy-start.1 = (bf16[8,512]{1,0:T(8,128)(2,1)S(1)}, bf16[8,512]{1,0:T(8,128)(2,1)}, u32[]{:S(2)}) copy-start(bf16[8,512]{1,0:T(8,128)(2,1)} %param.25) | copy-start | bytes 24580
  7.2 65.3 %copy-start.2 = (bf16[8,512]{1,0:T(8,128)(2,1)S(1)}, bf16[8,512]{1,0:T(8,128)(2,1)}, u32[]{:S(2)}) copy-start(bf16[8,512]{1,0:T(8,128)(2,1)} %param.26) | copy-start | bytes 24580
  7.2 114.0 %copy-start.3 = (s32[8]{0:T(128)S(1)}, s32[8]{0:T(128)}, u32[]{:S(2)}) copy-start(s32[8]{0:T(128)} %param.27) | copy-start | bytes 100
  7.2 118.7 %all-gather.9.cloned.1.call-start = ((), (), s32[]{:S(2)}) async-start(), calls=%async_computation | async-start | bytes 4325376 | tf_op jit(solution)/shard_map/all_gather | solution.py:148
  8.9 175.8 %all-gather.11.cloned.1.call-start = ((), (), s32[]{:S(2)}) async-start(), calls=%async_computation.1 | async-start | bytes 4325376 | tf_op jit(solution)/shard_map/all_gather | solution.py:149
  10.7 259.9 %all-gather.13.cloned.1.call-start = ((), (), s32[]{:S(2)}) async-start(), calls=%async_computation.2 | async-start | bytes 4325376 | tf_op jit(solution)/shard_map/all_gather | solution.py:167
  13.5 1.8 collective-permute-start
  17.0 339.3 %all-gather.15.cloned.1.call-start = ((), (), s32[]{:S(2)}) async-start(), calls=%async_computation.3 | async-start | bytes 4325376 | tf_op jit(solution)/shard_map/all_gather | solution.py:168
  446.1 1.9 copy-start
Sparse Core Ops, SparseCore 0:
  11.1 87.9 all-gather.8
  102.0 82.6 all-gather.10
  187.2 83.3 all-gather.12
  272.9 83.3 all-gather.14
where the time goes:
time: 457 us; the launch traced here: 456 us
  waiting for transfers between devices  219 us (48%)
  blocking collectives  99 us (22%)
  matrix products  57.8 us (13%)
  other arithmetic  31.9 us (7%)
  local copies, waits for them, and re-layouts  27 us (6%)
  between operations  16.2 us (4%)
  loops' own time  5.74 us (1%)
    all_gather x1, waiting for transfers between devices, local(): lax.all_gather(as_sent(partner_values), 'section', axis=0, tiled=True)  85.7 us
    all_gather x1, waiting for transfers between devices, local(): lax.all_gather(as_sent(partner_keys), 'section', axis=0, tiled=True)  72.2 us
    all_gather x1, waiting for transfers between devices, local(): lax.all_gather(own_values, 'section', axis=0, tiled=True)  58.9 us
    all_gather x1, blocking collectives, local(): lax.all_gather(prefix_keys, 'section', axis=0, tiled=True)  51.7 us
    all_gather x1, blocking collectives, local(): lax.all_gather(prefix_values, 'section', axis=0, tiled=True)  47.3 us
    dot_general x10, matrix products, absorb(): jnp.einsum('kgqs,skd->kgqd', weights.astype(jnp.bfloat16), value_heads, p...  38.6 us
    reduce_sum x10, other arithmetic, absorb(): weight_total = weight_total * fading + jnp.sum(weights, axis=-1)  22.2 us
    dot_general x10, matrix products, absorb(): jnp.einsum('qkgd,skd->kgqs', query_heads, key_heads, preferred_element_ty...  19.2 us
  transfers between devices with their start and end apart: 5, of which 4 were waited for; matrix products, arithmetic and copies ran while one was open for 6% of the time, Pallas kernels for 0%

commit v1 on v0

v1 whole, which is shorter than its diff:
```python
import functools

import jax
import jax.numpy as jnp
from jax import lax
from jax.experimental import pallas as pl
from jax.experimental.pallas import tpu as pltpu
from jax.sharding import PartitionSpec as P

QH = 32
KVH = 4
DH = 128
G = QH // KVH
NY = 4
NZ = 8
ROWS = 128
BLK = NY * ROWS
PRE_ROWS = 8
PIECE = 2 * PRE_ROWS
OWN_ROWS = 2 * BLK + NY * PIECE
HALF = OWN_ROWS // 2
NEGATIVE = -1e30
SCALE2 = DH ** -0.5 * 1.4426950408889634
SAFE = 100.0
NT = (((1,), (1,)), ((), ()))
f32 = jnp.float32
bf16 = jnp.bfloat16
VMEM = pltpu.VMEM


def at_section(z, y):
    return {"section": z * NY + y}


def gather_kernel(distance, q_ref, k_ref, v_ref, pk_ref, pv_ref, qh, own, par, pre,
                  local_sem, a2a_send, a2a_recv, ring_send, ring_recv):
    slot = lax.axis_index("pair")
    section = lax.axis_index("section")
    z = section // NY
    y = section % NY
    up = lax.rem(z + 1, NZ)
    down = lax.rem(z + NZ - 1, NZ)
    other = {"pair": slot ^ distance}

    def zb(step):
        return lax.rem(z + step + NZ, NZ)

    barrier = pltpu.get_barrier_semaphore()
    targets = [at_section(z, lax.rem(y + d, NY)) for d in range(1, NY)]
    targets += [at_section(up, y), at_section(down, y), other]
    for target in targets:
        pl.semaphore_signal(barrier, inc=1, device_id=target, device_id_type=pl.DeviceIdType.MESH)
    pre[...] = jnp.concatenate([pk_ref[...].astype(f32), pv_ref[...].astype(f32)], axis=0).astype(bf16)
    pl.semaphore_wait(barrier, len(targets))

    def heads(ref, width, head):
        return ref.at[:, pl.ds(pl.multiple_of(head * width, 128), width)]

    def places(head):
        return [
            (heads(k_ref, DH, head), own.at[z, pl.ds(y * ROWS, ROWS)]),
            (heads(v_ref, DH, head), own.at[z, pl.ds(BLK + y * ROWS, ROWS)]),
            (heads(pre, DH, head), own.at[z, pl.ds(2 * BLK + y * PIECE, PIECE)]),
            (heads(q_ref, G * DH, head), qh.at[y]),
        ]

    copies = []
    for d in range(1, NY):
        head = lax.rem(y + d, NY)
        for i, (src, dst) in enumerate(places(head)):
            copies.append(pltpu.make_async_remote_copy(
                src_ref=src, dst_ref=dst, send_sem=a2a_send.at[d - 1, i], recv_sem=a2a_recv.at[d - 1, i],
                device_id=at_section(z, head), device_id_type=pl.DeviceIdType.MESH))
    kv_copies = [c for i, c in enumerate(copies) if i % 4 != 3]
    q_copies = [c for i, c in enumerate(copies) if i % 4 == 3]
    locals_ = [pltpu.make_async_copy(src, dst, local_sem.at[i]) for i, (src, dst) in enumerate(places(y))]
    for c in kv_copies:
        c.start()
    for c in locals_:
        c.start()
    for c in q_copies:
        c.start()
    for c in locals_[:3]:
        c.wait()
    for c in kv_copies:
        c.wait_recv()

    ring = {}

    def send(name, src, dst, target):
        index = len(ring)
        copy = pltpu.make_async_remote_copy(
            src_ref=src, dst_ref=dst, send_sem=ring_send.at[index], recv_sem=ring_recv.at[index],
            device_id=target, device_id_type=pl.DeviceIdType.MESH)
        copy.start()
        ring[name] = copy

    to_up = at_section(up, y)
    to_down = at_section(down, y)

    def whole(name, step, target):
        send(name, own.at[zb(step)], own.at[zb(step)], target)

    def cross(name, step):
        part = pl.ds(0, 2 * BLK)
        send(name, own.at[zb(step), part], par.at[zb(step)], other)

    whole("u1", 0, to_up)
    whole("d1", 0, to_down)
    cross("x0", 0)
    ring["u1"].wait_recv()
    whole("u2", -1, to_up)
    cross("x-1", -1)
    ring["d1"].wait_recv()
    whole("d2", 1, to_down)
    cross("x+1", 1)
    ring["u2"].wait_recv()
    whole("u3", -2, to_up)
    cross("x-2", -2)
    ring["d2"].wait_recv()
    whole("d3", 2, to_down)
    cross("x+2", 2)
    ring["u3"].wait_recv()
    low = pl.ds(0, HALF)
    high = pl.ds(HALF, HALF)
    send("u4", own.at[zb(-3), low], own.at[zb(-3), low], to_up)
    ring["d3"].wait_recv()
    send("d4", own.at[zb(3), high], own.at[zb(3), high], to_down)
    ring["x-2"].wait_recv()
    send("pu3", par.at[zb(-2)], par.at[zb(-2)], to_up)
    ring["x+2"].wait_recv()
    send("pd3", par.at[zb(2)], par.at[zb(2)], to_down)
    low = pl.ds(0, BLK)
    high = pl.ds(BLK, BLK)
    ring["pu3"].wait_recv()
    send("pu4", par.at[zb(-3), low], par.at[zb(-3), low], to_up)
    ring["pd3"].wait_recv()
    send("pd4", par.at[zb(3), high], par.at[zb(3), high], to_down)
    for name in ("x0", "x-1", "x+1", "u4", "d4", "pu4", "pd4"):
        ring[name].wait_recv()
    locals_[3].wait()
    for c in q_copies:
        c.wait_recv()
    for c in copies:
        c.wait_send()
    for c in ring.values():
        c.wait_send()


def gather(distance, q, k, v, pk, pv):
    vmem = pl.BlockSpec(memory_space=VMEM)
    return pl.pallas_call(
        functools.partial(gather_kernel, distance),
        out_shape=(
            jax.ShapeDtypeStruct((NY, ROWS, G * DH), bf16),
            jax.ShapeDtypeStruct((NZ, OWN_ROWS, DH), bf16),
            jax.ShapeDtypeStruct((NZ, 2 * BLK, DH), bf16),
        ),
        in_specs=[vmem] * 5,
        out_specs=(vmem,) * 3,
        scratch_shapes=[
            VMEM((PIECE, KVH * DH), bf16),
            pltpu.SemaphoreType.DMA((4,)),
            pltpu.SemaphoreType.DMA((NY - 1, 4)),
            pltpu.SemaphoreType.DMA((NY - 1, 4)),
            pltpu.SemaphoreType.DMA((17,)),
            pltpu.SemaphoreType.DMA((17,)),
        ],
        compiler_params=pltpu.CompilerParams(
            collective_id=distance, has_side_effects=True, vmem_limit_bytes=32 << 20),
        name=f"gather_{distance}",
    )(q, k, v, pk, pv)


def attend_kernel(sc, qh, own, par, first, second, pk, pv, acc, total, top):
    z = sc[0]
    own_length = sc[1]
    partner_length = sc[2]

    def query(g):
        return qh[:, :, pl.ds(pl.multiple_of(g * DH, DH), DH)].reshape(BLK, DH)

    def own_kv(b):
        return own[b, pl.ds(0, BLK)], own[b, pl.ds(BLK, BLK)]

    def par_kv(b):
        return par[b, pl.ds(0, BLK)], par[b, pl.ds(BLK, BLK)]

    def causal():
        row = lax.broadcasted_iota(jnp.int32, (BLK, BLK), 0)
        return lax.broadcasted_iota(jnp.int32, (BLK, BLK), 1) <= row

    def before(limit):
        return lax.broadcasted_iota(jnp.int32, (BLK, BLK), 1) < limit

    full = partner_length // BLK
    rest = partner_length - full * BLK

    def store(ref, g, u):
        row = lax.broadcasted_iota(jnp.int32, (BLK, 1), 0) + z * BLK
        weight = jnp.sum(total[u], axis=1, keepdims=True)
        mixed = jnp.where(row < own_length, acc[u] / weight, 0.0).astype(bf16)
        ref[:, :, pl.ds(pl.multiple_of(g * DH, DH), DH)] = mixed.reshape(NY, ROWS, DH)

    def lanes(p):
        return sum(p[:, i * DH:(i + 1) * DH] for i in range(p.shape[1] // DH))

    def tile(g, parts):
        q = query(g)
        a = None
        t = None
        for keys, values, mask in parts:
            s = lax.dot_general(q, keys, NT, preferred_element_type=f32)
            p = jnp.exp2(s * SCALE2)
            if mask is not None:
                p = jnp.where(mask, p, 0.0)
            one = lanes(p)
            mixed = jnp.dot(p.astype(bf16), values, preferred_element_type=f32)
            a = mixed if a is None else a + mixed
            t = one if t is None else t + one
        return a, t

    def add(g, u, parts):
        a, t = tile(g, parts)
        acc[u] += a
        total[u] += t

    def span(pair, kv, count):
        def go(first_block, blocks):
            for u in range(2):
                add(pair * 2 + u, u, [kv(first_block + i) + (None,) for i in range(blocks)])

        def four(i, carry):
            go(i * 4, 4)
            return carry

        lax.fori_loop(0, count // 4, four, 0)

        @pl.when(lax.rem(count // 2, 2) == 1)
        def _():
            go(count // 4 * 4, 2)

        @pl.when(lax.rem(count, 2) == 1)
        def _():
            go(count - 1, 1)

    def fast():
        def one_pair(pair, carry):
            for u in range(2):
                g = pair * 2 + u
                acc[u], total[u] = tile(g, [(pk[...], pv[...], None), own_kv(z) + (causal(),)])
            span(pair, own_kv, z)
            for u in range(2):
                store(first, pair * 2 + u, u)
            span(pair, par_kv, full)

            @pl.when(rest > 0)
            def _():
                for u in range(2):
                    add(pair * 2 + u, u, [par_kv(full) + (before(rest),)])

            for u in range(2):
                store(second, pair * 2 + u, u)
            return carry

        lax.fori_loop(0, G // 2, one_pair, 0)

    def slow():
        def absorb(g, keys, values, mask):
            s = lax.dot_general(query(g), keys, NT, preferred_element_type=f32)
            if mask is not None:
                s = jnp.where(mask, s, NEGATIVE)
            now = jnp.maximum(top[...], jnp.max(s, axis=1, keepdims=True))
            fade = jnp.exp2((top[...] - now) * SCALE2)
            p = jnp.exp2((s - now[:, :1]) * SCALE2)
            if mask is not None:
                p = jnp.where(mask, p, 0.0)
            top[...] = now
            total[0] = total[0] * fade + lanes(p)
            acc[0] = acc[0] * fade + jnp.dot(p.astype(bf16), values, preferred_element_type=f32)

        def one_head(g, carry):
            top[...] = jnp.full_like(top, NEGATIVE)
            total[0] = jnp.zeros((BLK, DH), f32)
            acc[0] = jnp.zeros((BLK, DH), f32)
            absorb(g, pk[...], pv[...], None)
            absorb(g, *own_kv(z), causal())

            def own_block(b, c):
                absorb(g, *own_kv(b), None)
                return c

            def par_block(b, c):
                absorb(g, *par_kv(b), None)
                return c

            lax.fori_loop(0, z, own_block, 0)
            store(first, g, 0)
            lax.fori_loop(0, full, par_block, 0)

            @pl.when(rest > 0)
            def _():
                absorb(g, *par_kv(full), before(rest))

            store(second, g, 0)
            return carry

        lax.fori_loop(0, G, one_head, 0)

    def norm2(x):
        x = x.astype(f32)
        ones = jnp.ones((DH, DH), bf16)
        return jnp.max(jnp.dot((x * x).astype(bf16), ones, preferred_element_type=f32), axis=0, keepdims=True)

    needed = z * BLK < own_length

    @pl.when(jnp.logical_not(needed))
    def _():
        first[...] = jnp.zeros_like(first)
        second[...] = jnp.zeros_like(second)

    @pl.when(needed)
    def _():
        for b in range(NZ):
            piece = own[b, pl.ds(2 * BLK, NY * PIECE)].astype(f32).reshape(NY, 2, PRE_ROWS, DH)
            rows = pl.ds(b * NY * PRE_ROWS, NY * PRE_ROWS)
            pk[rows] = piece[:, 0].reshape(NY * PRE_ROWS, DH).astype(bf16)
            pv[rows] = piece[:, 1].reshape(NY * PRE_ROWS, DH).astype(bf16)

        q_norm = functools.reduce(jnp.maximum, [norm2(query(g)) for g in range(G)])
        k_norm = norm2(pk[...])
        for b in range(NZ):
            k_norm = jnp.maximum(k_norm, jnp.maximum(norm2(own_kv(b)[0]), norm2(par_kv(b)[0])))
        bound = jnp.max(q_norm) * jnp.max(k_norm)
        safe = bound * (1.02 * SCALE2 * SCALE2) < SAFE * SAFE

        @pl.when(safe)
        def _():
            fast()

        @pl.when(jnp.logical_not(safe))
        def _():
            slow()


def attend(sc, qh, own, par):
    vmem = pl.BlockSpec(memory_space=VMEM)
    out = jax.ShapeDtypeStruct((NY, ROWS, G * DH), bf16)
    return pl.pallas_call(
        attend_kernel,
        out_shape=(out, out),
        in_specs=[pl.BlockSpec(memory_space=pltpu.SMEM), vmem, vmem, vmem],
        out_specs=(vmem, vmem),
        scratch_shapes=[
            VMEM((NZ * NY * PRE_ROWS, DH), bf16),
            VMEM((NZ * NY * PRE_ROWS, DH), bf16),
            VMEM((2, BLK, DH), f32),
            VMEM((2, BLK, DH), f32),
            VMEM((BLK, DH), f32),
        ],
        compiler_params=pltpu.CompilerParams(vmem_limit_bytes=48 << 20),
        name="attend",
    )(sc, qh, own, par)


def scatter_kernel(first, second, out1, out2, local_sem, send_sem, recv_sem):
    section = lax.axis_index("section")
    z = section // NY
    y = section % NY
    barrier = pltpu.get_barrier_semaphore()
    for d in range(1, NY):
        pl.semaphore_signal(barrier, inc=1, device_id=at_section(z, lax.rem(y + d, NY)),
                            device_id_type=pl.DeviceIdType.MESH)
    pl.semaphore_wait(barrier, NY - 1)
    mine = pl.ds(pl.multiple_of(y * G * DH, DH), G * DH)
    copies = []
    for i, (src, dst) in enumerate(((first, out1), (second, out2))):
        for d in range(1, NY):
            to = lax.rem(y + d, NY)
            copies.append(pltpu.make_async_remote_copy(
                src_ref=src.at[to], dst_ref=dst.at[:, mine], send_sem=send_sem.at[i, d - 1],
                recv_sem=recv_sem.at[i, d - 1], device_id=at_section(z, to),
                device_id_type=pl.DeviceIdType.MESH))
        copies.append(pltpu.make_async_copy(src.at[y], dst.at[:, mine], local_sem.at[i]))
    for c in copies:
        c.start()
    for c in copies:
        c.wait()


def scatter(first, second):
    vmem = pl.BlockSpec(memory_space=VMEM)
    out = jax.ShapeDtypeStruct((ROWS, QH * DH), bf16)
    return pl.pallas_call(
        scatter_kernel,
        out_shape=(out, out),
        in_specs=[vmem, vmem],
        out_specs=(vmem, vmem),
        scratch_shapes=[
            pltpu.SemaphoreType.DMA((2,)),
            pltpu.SemaphoreType.DMA((2, NY - 1)),
            pltpu.SemaphoreType.DMA((2, NY - 1)),
        ],
        compiler_params=pltpu.CompilerParams(
            collective_id=8, has_side_effects=True, vmem_limit_bytes=32 << 20),
        name="scatter",
    )(first, second)


def local(queries, keys, values, prefix_keys, prefix_values, lengths, partner):
    slot = lax.axis_index("pair")
    section = lax.axis_index("section")
    partner_slot = partner[slot]
    distance = jnp.bitwise_xor(partner[0], 0)
    branches = [functools.partial(gather, d) for d in range(1, 8)]
    qh, own, par = lax.switch(
        distance - 1, branches, queries[0], keys[0], values[0], prefix_keys, prefix_values)
    sc = jnp.stack([section // NY, lengths[slot], lengths[partner_slot]]).astype(jnp.int32)
    first, second = attend(sc, qh, own, par)
    out1, out2 = scatter(first, second)
    return out1[None], out2[None]


def solution(mesh):
    in_specs = (
        P("pair", "section", None),
        P("pair", "section", None),
        P("pair", "section", None),
        P("section", None),
        P("section", None),
        P(),
        P(),
    )
    out_specs = (P("pair", "section", None), P("pair", "section", None))
    return jax.shard_map(local, mesh=mesh, in_specs=in_specs, out_specs=out_specs, check_vma=False)
```

time: 457 us -> 187 us (0.41)
  the two profiles are of different devices: /device:TPU:18 before, /device:TPU:225 now
where the time goes in v1:
time: 187 us; the launch traced here: 186 us
  Pallas kernels  177 us (95%)
  local copies, waits for them, and re-layouts  4.59 us (2%)
  between operations  3.26 us (2%)
    pallas_call x1, Pallas kernels, attend(): pl.pallas_call(attend_kernel, out_shape=(out, out), in_specs=[pl.BlockSpe...  113 us
    pallas_call x1, Pallas kernels, gather(): pl.pallas_call(functools.partial(gather_kernel, distance), out_shape=(jax...  48.6 us
    pallas_call x1, Pallas kernels, scatter(): pl.pallas_call(scatter_kernel, out_shape=(out, out), in_specs=[vmem, vmem...  16.1 us

profile of v1, /device:TPU:225, one launch (start us, length us, event | category | flops | bytes accessed | tf_op | source)
XLA Modules:
  0.0 186.5 jit_solution(6034230190521463687)
XLA Ops:
  0.6 1.3 fusion
  4.6 1.3 fusion.1
  5.9 1.4 pad_add_fusion.sc
  7.3 48.6 %conditional.1 = ((bf16[4,128,1024]{2,1,0:T(8,128)(2,1)S(1)}, bf16[8,1088,128]{2,1,0:T(8,128)(2,1)S(1)}, bf16[8,1024,128]{2,1,0:T(8,128)(2,1)})) conditional(s32[]{:T(128)} %bitcast.2, (bf16[128,4096]{1,0:T(8,128)(2,1)}, bf16[128,512]{1,0:T(8,128)(2,1)}, bf16[128,512]{1,0:T(8,128)(2,1)}, bf16[8,512]{1,0:T(8,128)(2,1)}, ...), branch_computations={%region_0.0_spmd, %region_1.0_spmd, %region_2.0_spmd, %region_3.0_... | conditional | bytes 8 | solution.py:416
  7.3 48.6 %gather_6.1 = (bf16[4,128,1024]{2,1,0:T(8,128)(2,1)S(1)}, bf16[8,1088,128]{2,1,0:T(8,128)(2,1)S(1)}, bf16[8,1024,128]{2,1,0:T(8,128)(2,1)}) custom-call(bf16[128,4096]{1,0:T(8,128)(2,1)} %get-tuple-element.95.q_ref, bf16[128,512]{1,0:T(8,128)(2,1)} %get-tuple-element.96.k_ref, bf16[128,512]{1,0:T(8,128)(2,1)} %get-tuple-element.97.v_ref, ...), custom_call_target="tpu_custom_call" | custom-call | tf_op jit(solution)/shard_map/cond/branch_5_fun/gather_6/pallas_call | solution.py:152
  55.8 112.6 %attend.1 = (bf16[4,128,1024]{2,1,0:T(8,128)(2,1)S(1)}, bf16[4,128,1024]{2,1,0:T(8,128)(2,1)S(1)}) custom-call(s32[3]{0:T(128)S(1)} %pad_add_fusion.sc, bf16[4,128,1024]{2,1,0:T(8,128)(2,1)S(1)} %get-tuple-element.114.qh, bf16[8,1088,128]{2,1,0:T(8,128)(2,1)S(1)} %get-tuple-element.115.own, bf16[8,1024,128]{2,1,0:T(8,128)(2,1)} %get-tuple-element.116.par), custom_call_target="tpu_custom_call" | custom-call | tf_op jit(solution)/shard_map/attend/pallas_call | solution.py:349
  168.4 16.1 %scatter.1 = (bf16[128,4096]{1,0:T(8,128)(2,1)S(1)}, bf16[128,4096]{1,0:T(8,128)(2,1)S(1)}) custom-call(bf16[4,128,1024]{2,1,0:T(8,128)(2,1)S(1)} %get-tuple-element.117.first, bf16[4,128,1024]{2,1,0:T(8,128)(2,1)S(1)} %get-tuple-element.118.second), custom_call_target="tpu_custom_call" | custom-call | tf_op jit(solution)/shard_map/scatter/pallas_call | solution.py:394
  184.5 1.0 copy.32
  185.5 1.0 copy.33
